TPU v7x, 256 devices: a whole 4x4x8 slice. The times are simulated.
256 devices in a mesh: dp: 16 (over y, x_hi, core), tensor: 16 (over x_lo, z).
Axes of the slice: x: 4 (x_hi: 2, x_lo: 2; x = x_hi * 2 + x_lo), y: 4, z: 8, core: 2. Of those that a mesh axis runs over, the one named last changes fastest.
Arguments:
- gate_pre: bfloat16 [8192, 18432], P('dp', 'tensor'), may hold values from -6 to 6
- up_saved: bfloat16 [8192, 18432], P('dp', 'tensor'), may hold values from -6 to 6
- cotangent: bfloat16 [8192, 4608], P(('dp', 'tensor')), may hold values from -24 to 24
- down_weight: bfloat16 [4608, 18432], P('dp', 'tensor'), may hold values from -0.046875 to 0.046875
Outputs:
- grad_gate: bfloat16 [8192, 18432], P('dp', 'tensor')
- grad_up: bfloat16 [8192, 18432], P('dp', 'tensor')
- grad_down: bfloat16 [4608, 18432], P('dp', 'tensor')
All inputs are finite; a program needn't handle non-finite values.
Results may differ from a plain program's by a relative error of at most 0.017.
Values may be sent and summed in bfloat16 or wider, within the bound.
A program may use at most 128 MiB of HBM per device.

v0:
```python
import jax
import jax.numpy as jnp
from jax import lax
from jax.sharding import PartitionSpec as P

root_coef = 0.7978845608028654
cubic_coef = 0.044715


def gelu_parts(gate_f32):
    inner = root_coef * (gate_f32 + cubic_coef * gate_f32 * gate_f32 * gate_f32)
    tanh_val = jnp.tanh(inner)
    activated = 0.5 * gate_f32 * (1.0 + tanh_val)
    derivative = 0.5 * (1.0 + tanh_val) + 0.5 * gate_f32 * (
        1.0 - tanh_val * tanh_val
    ) * root_coef * (1.0 + 3.0 * cubic_coef * gate_f32 * gate_f32)
    return (activated, derivative)


def on_device(gate_pre, up_saved, cotangent, down_weight):
    gate_f32 = gate_pre.astype(jnp.float32)
    up_f32 = up_saved.astype(jnp.float32)
    activated, derivative = gelu_parts(gate_f32)
    hidden = (activated * up_f32).astype(jnp.bfloat16)
    cot_full = lax.all_gather(cotangent, "tensor", axis=0, tiled=True)
    columns = cot_full
    grad_hidden = jnp.dot(
        columns,
        lax.all_gather(down_weight, "dp", axis=0, tiled=True),
        preferred_element_type=jnp.float32,
    )
    grad_gate = (grad_hidden * up_f32 * derivative).astype(jnp.bfloat16)
    grad_up = (grad_hidden * activated).astype(jnp.bfloat16)
    columns = cot_full
    grad_down = lax.psum_scatter(
        lax.dot_general(
            columns, hidden, (((0,), (0,)), ((), ())), preferred_element_type=jnp.float32
        ).astype(jnp.bfloat16),
        "dp",
        scatter_dimension=0,
        tiled=True,
    )
    return (grad_gate, grad_up, grad_down)


def solution(mesh):
    in_specs = (P("dp", "tensor"), P("dp", "tensor"), P(("dp", "tensor"), None), P("dp", "tensor"))
    out_specs = (P("dp", "tensor"), P("dp", "tensor"), P("dp", "tensor"))
    return jax.shard_map(
        on_device, mesh=mesh, in_specs=in_specs, out_specs=out_specs, check_vma=False
    )
```

profile of v0, /device:TPU:1, one launch (start us, length us, event | category | flops | bytes accessed | tf_op | source)
XLA Modules:
  0.0 308.6 jit_solution(2480499893650493027)
XLA Ops:
  7.2 0.0 all-gather.3.cloned.1.call-start
  7.2 0.7 all-gather.3.cloned.1.call-update
  7.9 0.0 all-gather.5.cloned.1.call-start
  7.9 0.7 all-gather.5.cloned.1.call-update
  8.6 0.0 reduce-scatter.4.cloned.1.call-start
  8.7 74.1 %all-gather.3.cloned.1.call-done = bf16[512,4608]{1,0:T(8,128)(2,1)} async-done(((bf16[32,4608]{1,0:T(8,128)(2,1)}), bf16[512,4608]{1,0:T(8,128)(2,1)}) %all-gather.3.cloned.1.call-update) | async-done | bytes 4718608 | tf_op jit(solution)/shard_map/all_gather | solution.py:25
  82.8 11.6 %fusion = bf16[4608,1152]{0,1:T(8,128)(2,1)} fusion(bf16[512,4608]{1,0:T(8,128)(2,1)} %all-gather.3.cloned.1.call-done, bf16[512,1152]{1,0:T(8,128)(2,1)} %param.5, bf16[512,1152]{1,0:T(8,128)(2,1)} %param.4), kind=kOutput, calls=%fused_computation.1 | convolution fusion | flops 5448204288 | bytes 17694720 | tf_op jit(solution)/shard_map/dot_general | solution.py:36
  94.4 14.8 %copy.9 = bf16[4608,1152]{1,0:T(8,128)(2,1)} copy(bf16[4608,1152]{0,1:T(8,128)(2,1)} %fusion) | data formatting | bytes 21233664
  109.2 0.0 copy-start
  109.2 0.0 copy-start.1
  109.2 0.0 reduce-scatter.4.cloned.1.call-update
  109.2 70.3 %all-gather.5.cloned.1.call-done = bf16[4608,1152]{1,0:T(8,128)(2,1)} async-done(((bf16[288,1152]{1,0:T(8,128)(2,1)}), bf16[4608,1152]{1,0:T(8,128)(2,1)}) %all-gather.5.cloned.1.call-update) | async-done | bytes 10616848 | tf_op jit(solution)/shard_map/all_gather | solution.py:29
  179.5 0.0 copy-done
  179.5 0.0 copy-done.1
  179.5 13.3 %multiply_convert_fusion = (bf16[512,1152]{1,0:T(8,128)(2,1)}, bf16[512,1152]{1,0:T(8,128)(2,1)}) fusion(bf16[512,1152]{1,0:T(8,128)(2,1)S(1)} %copy-done, bf16[512,1152]{1,0:T(8,128)(2,1)S(1)} %copy-done.1, bf16[512,4608]{1,0:T(8,128)(2,1)} %all-gather.3.cloned.1.call-done, bf16[4608,1152]{1,0:T(8,128)(2,1)} %all-gather.5.cloned.1.call-done), kind=kOutput, calls=%fused_computation.22 | convolution fusion | flops 5450563584 | bytes 20054016 | tf_op jit(solution)/shard_map/dot_general | solution.py:27
  192.8 109.2 %reduce-scatter.4.cloned.1.call-done = bf16[288,1152]{1,0:T(8,128)(2,1)} async-done(((bf16[4608,1152]{1,0:T(8,128)(2,1)}), bf16[288,1152]{1,0:T(8,128)(2,1)}) %reduce-scatter.4.cloned.1.call-update) | async-done | bytes 663568
Async XLA Ops:
  7.2 75.6 %all-gather.3.cloned.1.call-start = ((), (), s32[]{:S(2)}) async-start(), calls=%async_computation.1 | async-start | bytes 5013504 | tf_op jit(solution)/shard_map/all_gather | solution.py:25
  7.9 171.6 %all-gather.5.cloned.1.call-start = ((), (), s32[]{:S(2)}) async-start(), calls=%async_computation.2 | async-start | bytes 11280384 | tf_op jit(solution)/shard_map/all_gather | solution.py:29
  8.6 293.4 %reduce-scatter.4.cloned.1.call-start = ((), (), s32[]{:S(2)}) async-start(), calls=%async_computation.3 | async-start | bytes 11280384
  109.2 70.3 %copy-start = (bf16[512,1152]{1,0:T(8,128)(2,1)S(1)}, bf16[512,1152]{1,0:T(8,128)(2,1)}, u32[]{:S(2)}) copy-start(bf16[512,1152]{1,0:T(8,128)(2,1)} %param.4) | copy-start | bytes 3538948
  109.2 70.3 %copy-start.1 = (bf16[512,1152]{1,0:T(8,128)(2,1)S(1)}, bf16[512,1152]{1,0:T(8,128)(2,1)}, u32[]{:S(2)}) copy-start(bf16[512,1152]{1,0:T(8,128)(2,1)} %param.5) | copy-start | bytes 3538948
Sparse Core Ops, SparseCore 0:
  9.8 72.9 all-gather.2
  85.5 93.9 all-gather.4
  184.7 117.2 reduce-scatter.3
where the time goes:
time: 309 us
  waiting for transfers between devices  255 us (83%)
  matrix products  24.9 us (8%)
  local copies, waits for them, and re-layouts  14.8 us (5%)
  between operations  13.7 us (4%)
    unnamed x4, waiting for transfers between devices  111 us
    all_gather x1, waiting for transfers between devices, on_device(): cot_full = lax.all_gather(cotangent, 'tensor', axis=0, tiled=True)  74.1 us
    all_gather x1, waiting for transfers between devices, on_device(): lax.all_gather(down_weight, 'dp', axis=0, tiled=True)  70.3 us
    unnamed x5, local copies, waits for them, and re-layouts  14.8 us
    dot_general x1, matrix products, on_device(): jnp.dot(columns, lax.all_gather(down_weight, 'dp', axis=0, tiled=True), p...  13.3 us
    dot_general x1, matrix products, on_device(): lax.dot_general(columns, hidden, (((0,), (0,)), ((), ())), preferred_elem...  11.6 us
  transfers between devices with their start and end apart: 3, of which 3 were waited for; matrix products, arithmetic and copies ran while one was open for 13% of the time, Pallas kernels for 0%

commit v1 on v0

v1 whole, which is shorter than its diff:
```python
import functools

import jax
import jax.numpy as jnp
from jax import lax
from jax.experimental import pallas as pl
from jax.experimental.pallas import tpu as pltpu
from jax.sharding import PartitionSpec as P

MESH = pl.DeviceIdType.MESH
BF16, F32 = jnp.bfloat16, jnp.float32

root_coef = 0.7978845608028654
cubic_coef = 0.044715

D = 4608
FF = 1152
ROWS = 32
QD = 1152
OWN = 288
HALF = OWN // 2
TILE = 384
ORDER = (2, 1, 3, 0)
POS = {r: p for p, r in enumerate(ORDER)}
SUBS = (0, 1, 3, 2)
ROUNDS = ((0, 3), (3, 2), (5, 2), (7, 1))


def gelu_parts(gate_f32):
    inner = root_coef * (gate_f32 + cubic_coef * gate_f32 * gate_f32 * gate_f32)
    tanh_val = jnp.tanh(inner)
    activated = 0.5 * gate_f32 * (1.0 + tanh_val)
    derivative = 0.5 * (1.0 + tanh_val) + 0.5 * gate_f32 * (
        1.0 - tanh_val * tanh_val
    ) * root_coef * (1.0 + 3.0 * cubic_coef * gate_f32 * gate_f32)
    return (activated, derivative)


def kernel(
    gate, up, cot, weight, grad_gate, grad_up, grad_down,
    csrc, cbuf, wbuf, hbuf, act, uder, acc,
    peer_out, peer_in, kept, far_out, far_in, gd_out, gd_half, gd_in,
    c_s, c_r, z_s, z_r, w_s, w_r, h_s, h_r, p_s, p_r, f_s, f_r, g_s, g_r,
):
    dp, tensor = lax.axis_index("dp"), lax.axis_index("tensor")
    y, xh, c = dp // 4, (dp // 2) % 2, dp % 2
    xl, z = tensor // 8, tensor % 8
    x = xh * 2 + xl

    def at(dx=0, dy=0, dz=0, dc=0):
        nx, ny, nz, nc = (x + dx) % 4, (y + dy) % 4, (z + dz) % 8, (c + dc) % 2
        return (ny * 4 + (nx // 2) * 2 + nc, (nx % 2) * 8 + nz)

    started = []

    def send(src, dst, ss, rs, to):
        copy = pltpu.make_async_remote_copy(
            src_ref=src, dst_ref=dst, send_sem=ss, recv_sem=rs, device_id=to, device_id_type=MESH
        )
        copy.start()
        started.append(copy)
        return copy

    near = [(dx, dc) for dx in range(4) for dc in range(2) if (dx, dc) != (0, 0)]
    barrier = pltpu.get_barrier_semaphore()
    partners = [at(dx=dx, dc=dc) for dx, dc in near] + [at(dz=1), at(dz=7), at(dy=1), at(dy=3)]
    for partner in partners:
        pl.semaphore_signal(barrier, inc=1, device_id=partner, device_id_type=MESH)

    for p, r in enumerate(ORDER):
        start = pl.multiple_of(((y + r) % 4) * QD, 128)
        block = cot[:, pl.ds(start, QD)]
        for q in range(4):
            csrc[q, :, p * OWN : (p + 1) * OWN] = block[:, q * OWN : (q + 1) * OWN]
    wbuf[pl.ds(POS[0] * OWN, OWN), :] = weight[...]
    cbuf[0, c, x] = csrc[xh * 2 + c]

    pl.semaphore_wait(barrier, len(partners))

    c_copies = {}
    for i, (dx, dc) in enumerate(near):
        nq = (((x + dx) % 4) // 2) * 2 + (c + dc) % 2
        c_copies[dx, dc] = send(
            csrc.at[nq], cbuf.at[0, c, x], c_s.at[i], c_r.at[i], at(dx=dx, dc=dc)
        )

    def wrows(r, first=0, rows=OWN):
        return wbuf.at[pl.ds(POS[r] * OWN + first, rows)]

    w_up = send(wrows(0), wrows(3), w_s.at[0], w_r.at[0], at(dy=1))
    w_down = send(wrows(0), wrows(1), w_s.at[1], w_r.at[1], at(dy=3))

    def z_of(slot):
        return (z + (1 - 2 * (slot % 2)) * ((slot + 1) // 2) + 8) % 8

    def hidden(slot, _):
        zs = z_of(slot)
        up_f32 = up[:, zs].astype(F32)
        activated, derivative = gelu_parts(gate[:, zs].astype(F32))
        act[slot] = activated
        uder[slot] = up_f32 * derivative
        hbuf[slot, c, pl.ds(xh * 2, 2)] = (activated * up_f32).astype(BF16)
        return 0

    def ring(step, j):
        xs = (x + SUBS[j]) % 4
        out = []
        for way in range(2):
            if step == 3 and (j < 2) != (way == 0):
                out.append(None)
                continue
            src = 0 if step == 0 else 2 * step - 1 + way
            dst = 7 if step == 3 else 2 * step + 1 + way
            out.append(
                send(
                    cbuf.at[src, :, xs], cbuf.at[dst, :, xs],
                    z_s.at[way, step, j], z_r.at[way, step, j],
                    at(dz=1 if way == 0 else 7),
                )
            )
        return out

    ringed = {}

    def arrive(step, j):
        for copy in ringed[step, j]:
            if copy is not None:
                copy.wait_recv()

    def forward(step):
        for j in range(4):
            arrive(step - 1, j)
            ringed[step, j] = ring(step, j)

    h_copies = {}

    def send_h(i):
        mine = hbuf.at[pl.ds(2 * i, 2), c, pl.ds(xh * 2, 2)]
        h_copies["p", i] = send(mine, mine, h_s.at[0, i], h_r.at[0, i], at(dc=1))
        h_copies["x", i] = send(mine, mine, h_s.at[1, i], h_r.at[1, i], at(dx=2))

    def pass_h(i):
        h_copies["x", i].wait_recv()
        theirs = hbuf.at[pl.ds(2 * i, 2), c, pl.ds((1 - xh) * 2, 2)]
        h_copies["f", i] = send(theirs, theirs, h_s.at[2, i], h_r.at[2, i], at(dc=1))

    def arrive_h(i):
        h_copies["p", i].wait_recv()
        h_copies["f", i].wait_recv()

    for j in range(4):
        lax.fori_loop(2 * j, 2 * j + 2, hidden, 0)
        dx = (4 - SUBS[j]) % 4
        for dc in range(2):
            if (dx, dc) != (0, 0):
                c_copies[dx, dc].wait_recv()
        ringed[0, j] = ring(0, j)
    for i in range(4):
        send_h(i)

    forward(1)
    w_up.wait_recv()
    w_up2 = send(wrows(3, 0, HALF), wrows(2, 0, HALF), w_s.at[2], w_r.at[2], at(dy=1))
    w_down.wait_recv()
    w_down2 = send(
        wrows(1, HALF, HALF), wrows(2, HALF, HALF), w_s.at[3], w_r.at[3], at(dy=3)
    )
    pass_h(0)

    def grad_hidden(first, n, cp, store):
        @pl.loop(0, FF // TILE)
        def _(t):
            cols = pl.ds(pl.multiple_of(t * TILE, TILE), TILE)
            lhs = cbuf[pl.ds(first, n), cp].reshape(n * 128, QD)
            out = jnp.dot(lhs, wbuf[:, cols], preferred_element_type=F32)
            store(cols, out.reshape(n, 4, ROWS, TILE))

    p_copies, f_copies = {}, {}

    def partial_hidden(i):
        first, n = ROUNDS[i]
        slots = pl.ds(first, n)

        def to_peer(cols, out):
            peer_out[slots, :, :, cols] = out.astype(BF16)

        def keep(cols, out):
            kept[slots, :, :, cols] = out

        grad_hidden(first, n, 1 - c, to_peer)
        p_copies[i] = send(
            peer_out.at[slots], peer_in.at[slots], p_s.at[i], p_r.at[i], at(dc=1)
        )
        grad_hidden(first, n, c, keep)

    def add_peer(i):
        first, n = ROUNDS[i]
        p_copies[i].wait_recv()

        def one(slot, _):
            far = pl.ds((1 - xh) * 2, 2)
            total = kept[slot, far] + peer_in[slot, far].astype(F32)
            far_out[slot] = total.astype(BF16)
            return 0

        lax.fori_loop(first, first + n, one, 0)
        slots = pl.ds(first, n)
        f_copies[i] = send(
            far_out.at[slots], far_in.at[slots], f_s.at[i], f_r.at[i], at(dx=2)
        )

    def finish_hidden(i):
        first, n = ROUNDS[i]
        f_copies[i].wait_recv()

        def one(slot, _):
            zs = z_of(slot)
            near_x = pl.ds(xh * 2, 2)
            total = (
                kept[slot, near_x]
                + peer_in[slot, near_x].astype(F32)
                + far_in[slot].astype(F32)
            )
            grad_gate[:, zs] = (total * uder[slot]).astype(BF16)
            grad_up[:, zs] = (total * act[slot]).astype(BF16)
            return 0

        lax.fori_loop(first, first + n, one, 0)

    def partial_down(i, tile):
        first, n = ROUNDS[i]
        rows = pl.ds(pl.multiple_of(tile * TILE, TILE), TILE)
        lhs = cbuf[pl.ds(first, n), :, :, :, rows].reshape(n * 256, TILE)
        for t in range(FF // TILE):
            cols = slice(t * TILE, (t + 1) * TILE)
            rhs = hbuf[pl.ds(first, n), :, :, :, cols].reshape(n * 256, TILE)
            out = lax.dot_general(lhs, rhs, (((0,), (0,)), ((), ())), preferred_element_type=F32)
            if i == 0:
                acc[rows, cols] = out
            else:
                acc[rows, cols] += out

    def down_round(i):
        @pl.loop(0, QD // TILE)
        def _(tile):
            partial_down(i, tile)

    ringed[2, 0] = None
    for j in range(2):
        arrive(1, j)
        ringed[2, j] = ring(2, j)
    pass_h(1)
    arrive_h(0)
    arrive_h(1)
    down_round(0)
    for j in range(2, 4):
        arrive(1, j)
        ringed[2, j] = ring(2, j)
    w_up2.wait_recv()
    w_down2.wait_recv()
    partial_hidden(0)
    add_peer(0)
    pass_h(2)
    partial_hidden(1)
    add_peer(1)
    for j in range(2):
        arrive(2, j)
        ringed[3, j] = ring(3, j)
    arrive_h(2)
    down_round(1)
    pass_h(3)
    for j in range(2, 4):
        arrive(2, j)
        ringed[3, j] = ring(3, j)
    partial_hidden(2)
    add_peer(2)
    arrive_h(3)
    down_round(2)
    for j in range(4):
        arrive(3, j)

    def gd_rows(r, first=0, rows=OWN):
        return pl.ds(POS[r] * OWN + first, rows)

    def round_gd(r):
        gd_out[gd_rows(r)] = acc[gd_rows(r), :].astype(BF16)

    g = {}

    def send_gd(name, k, rows, dst, to):
        g[name] = send(gd_out.at[rows], dst, g_s.at[k], g_r.at[k], to)

    upward, downward = at(dy=1), at(dy=3)
    partial_down(3, 0)
    round_gd(2)
    send_gd("u2", 0, gd_rows(2, 0, HALF), gd_half.at[0], upward)
    send_gd("d2", 1, gd_rows(2, HALF, HALF), gd_half.at[1], downward)
    partial_down(3, 1)
    round_gd(1)
    send_gd("u1", 2, gd_rows(1, HALF, HALF), gd_in.at[0, pl.ds(HALF, HALF)], upward)
    partial_down(3, 2)
    round_gd(3)
    send_gd("d1", 3, gd_rows(3, 0, HALF), gd_in.at[1, pl.ds(0, HALF)], downward)
    partial_hidden(3)
    add_peer(3)
    finish_hidden(0)
    g["u2"].wait_recv()
    rows = gd_rows(1, 0, HALF)
    gd_out[rows] = (acc[rows, :] + gd_half[0].astype(F32)).astype(BF16)
    send_gd("u3", 4, rows, gd_in.at[0, pl.ds(0, HALF)], upward)
    g["d2"].wait_recv()
    rows = gd_rows(3, HALF, HALF)
    gd_out[rows] = (acc[rows, :] + gd_half[1].astype(F32)).astype(BF16)
    send_gd("d3", 5, rows, gd_in.at[1, pl.ds(HALF, HALF)], downward)
    finish_hidden(1)
    finish_hidden(2)
    finish_hidden(3)
    g["u1"].wait_recv()
    g["d1"].wait_recv()
    g["u3"].wait_recv()
    g["d3"].wait_recv()
    grad_down[...] = (
        acc[gd_rows(0), :] + gd_in[0].astype(F32) + gd_in[1].astype(F32)
    ).astype(BF16)
    for copy in started:
        copy.wait_send()


def on_device(gate_pre, up_saved, cotangent, down_weight):
    vmem = pl.BlockSpec(memory_space=pltpu.VMEM)
    dma = pltpu.SemaphoreType.DMA
    tokens = (2, 8, ROWS, FF)
    grad_gate, grad_up, grad_down = pl.pallas_call(
        kernel,
        name="ffn_down_backward",
        out_shape=(
            jax.ShapeDtypeStruct(tokens, BF16),
            jax.ShapeDtypeStruct(tokens, BF16),
            jax.ShapeDtypeStruct((OWN, FF), BF16),
        ),
        in_specs=[vmem] * 4,
        out_specs=(vmem,) * 3,
        scratch_shapes=[
            pltpu.VMEM((4, ROWS, QD), BF16),
            pltpu.VMEM((8, 2, 4, ROWS, QD), BF16),
            pltpu.VMEM((QD, FF), BF16),
            pltpu.VMEM((8, 2, 4, ROWS, FF), BF16),
            pltpu.VMEM((8, 2, ROWS, FF), F32),
            pltpu.VMEM((8, 2, ROWS, FF), F32),
            pltpu.VMEM((QD, FF), F32),
            pltpu.VMEM((8, 4, ROWS, FF), BF16),
            pltpu.VMEM((8, 4, ROWS, FF), BF16),
            pltpu.VMEM((8, 4, ROWS, FF), F32),
            pltpu.VMEM((8, 2, ROWS, FF), BF16),
            pltpu.VMEM((8, 2, ROWS, FF), BF16),
            pltpu.VMEM((QD, FF), BF16),
            pltpu.VMEM((2, HALF, FF), BF16),
            pltpu.VMEM((2, OWN, FF), BF16),
            dma((7,)), dma((7,)),
            dma((2, 4, 4)), dma((2, 4, 4)),
            dma((4,)), dma((4,)),
            dma((3, 4)), dma((3, 4)),
            dma((4,)), dma((4,)),
            dma((4,)), dma((4,)),
            dma((6,)), dma((6,)),
        ],
        compiler_params=pltpu.CompilerParams(
            collective_id=0, has_side_effects=True, vmem_limit_bytes=60 << 20
        ),
        cost_estimate=pl.CostEstimate(
            flops=4 * 2048 * QD * FF, bytes_accessed=7 << 20, transcendentals=512 * FF
        ),
    )(
        gate_pre.reshape(tokens), up_saved.reshape(tokens), cotangent, down_weight
    )
    return (grad_gate.reshape(512, FF), grad_up.reshape(512, FF), grad_down)


def solution(mesh):
    in_specs = (P("dp", "tensor"), P("dp", "tensor"), P(("dp", "tensor"), None), P("dp", "tensor"))
    out_specs = (P("dp", "tensor"), P("dp", "tensor"), P("dp", "tensor"))
    return jax.shard_map(
        on_device, mesh=mesh, in_specs=in_specs, out_specs=out_specs, check_vma=False
    )
```

time: 309 us -> 95.9 us (0.31)
  waiting for transfers between devices: 255 us -> 0 us
  Pallas kernels: 0 us -> 90.3 us
  matrix products: 24.9 us -> 0 us
  between operations: 13.7 us -> 0.65 us
  local copies, waits for them, and re-layouts: 14.8 us -> 4.83 us
    all_gather x2 -> x0, waiting for transfers between devices: 144 us -> none  [the longest x1 74.1 us: on_device(): cot_full = lax.all_gather(cotangent, 'tensor', axis=0, tiled=True)]
    unnamed x4 -> x0, waiting for transfers between devices: 111 us -> none
    pallas_call x0 -> x1, Pallas kernels: none -> 90.3 us  [on_device(): pl.pallas_call(kernel, name='ffn_down_backward', out_shape=(jax.ShapeDtyp...]
    dot_general x2 -> x0, matrix products: 24.9 us -> none  [the longest x1 13.3 us: on_device(): jnp.dot(columns, lax.all_gather(down_weight, 'dp', axis=0, tiled=True), p...]
    unnamed x5 -> x7, local copies, waits for them, and re-layouts: 14.8 us -> 4.83 us
  transfers between devices with their start and end apart: 3 -> 0, of which waited for: 3 -> 0; matrix products, arithmetic and copies ran while one was open for 13% -> 0% of each run, Pallas kernels for 0% -> 0%
where the time goes in v1:
time: 95.9 us; the launch traced here: 95.7 us
  Pallas kernels  90.3 us (94%)
  local copies, waits for them, and re-layouts  4.83 us (5%)
    pallas_call x1, Pallas kernels, on_device(): pl.pallas_call(kernel, name='ffn_down_backward', out_shape=(jax.ShapeDtyp...  90.3 us
    unnamed x7, local copies, waits for them, and re-layouts  4.83 us

profile of v1, /device:TPU:1, one launch (start us, length us, event | category | flops | bytes accessed | tf_op | source)
XLA Modules:
  0.0 95.7 jit_solution(3023034053534855375)
XLA Ops:
  0.6 90.3 %ffn_down_backward.1 = (bf16[2,8,32,1152]{3,2,1,0:T(8,128)(2,1)}, bf16[2,8,32,1152]{3,2,1,0:T(8,128)(2,1)}, bf16[288,1152]{1,0:T(8,128)(2,1)}) custom-call(bf16[2,8,32,1152]{3,2,1,0:T(8,128)(2,1)} %bitcast.6, bf16[2,8,32,1152]{3,2,1,0:T(8,128)(2,1)} %bitcast.7, bf16[32,4608]{1,0:T(8,128)(2,1)} %cot.1, bf16[288,1152]{1,0:T(8,128)(2,1)} %weight.1), custom_call_target="tpu_custom_call" | custom-call | flops 10871635968 | bytes 7340032 | tf_op jit(solution)/shard_map/ffn_down_backward/pallas_call | solution.py:333
  90.9 0.0 copy-start
  90.9 2.5 %copy.10 = bf16[512,1152]{1,0:T(8,128)(2,1)} copy(bf16[512,1152]{1,0:T(8,128)(2,1)} %bitcast.5) | data formatting | bytes 2359296
  93.4 0.0 copy-done
  93.4 0.0 copy-start.1
  93.4 1.0 %copy.11 = bf16[512,1152]{1,0:T(8,128)(2,1)} copy(bf16[512,1152]{1,0:T(8,128)(2,1)S(1)} %bitcast.4) | data formatting | bytes 2359296
  94.4 0.5 copy-done.1
  94.9 0.8 copy.12
Async XLA Ops:
  90.9 2.5 %copy-start = (bf16[2,8,32,1152]{3,2,1,0:T(8,128)(2,1)S(1)}, bf16[2,8,32,1152]{3,2,1,0:T(8,128)(2,1)}, u32[]{:S(2)}) copy-start(bf16[2,8,32,1152]{3,2,1,0:T(8,128)(2,1)} %get-tuple-element.7) | copy-start | bytes 3538948
  93.4 1.5 %copy-start.1 = (bf16[288,1152]{1,0:T(8,128)(2,1)S(1)}, bf16[288,1152]{1,0:T(8,128)(2,1)}, u32[]{:S(2)}) copy-start(bf16[288,1152]{1,0:T(8,128)(2,1)} %get-tuple-element.14) | copy-start | bytes 1990660

commit v2 on v1

--- a/solution.py
+++ b/solution.py
@@ -23,7 +23,8 @@
 ORDER = (2, 1, 3, 0)
 POS = {r: p for p, r in enumerate(ORDER)}
 SUBS = (0, 1, 3, 2)
-ROUNDS = ((0, 3), (3, 2), (5, 2), (7, 1))
+ROUNDS = ((0, 3), (3, 2), (5, 3))
+CHUNKS = ((0, 384), (384, 256), (640, 256), (896, 256))
 
 
 def gelu_parts(gate_f32):
@@ -37,10 +38,10 @@
 
 
 def kernel(
-    gate, up, cot, weight, grad_gate, grad_up, grad_down,
-    csrc, cbuf, wbuf, hbuf, act, uder, acc,
+    gate_hbm, up_hbm, cot_hbm, weight, grad_gate, grad_up, grad_down,
+    gate, up, cot, csrc, cbuf, wbuf, hbuf, act, uder, acc,
     peer_out, peer_in, kept, far_out, far_in, gd_out, gd_half, gd_in,
-    c_s, c_r, z_s, z_r, w_s, w_r, h_s, h_r, p_s, p_r, f_s, f_r, g_s, g_r,
+    in_s, c_s, c_r, z_s, z_r, w_s, w_r, h_s, h_r, p_s, p_r, f_s, f_r, g_s, g_r,
 ):
     dp, tensor = lax.axis_index("dp"), lax.axis_index("tensor")
     y, xh, c = dp // 4, (dp // 2) % 2, dp % 2
@@ -67,26 +68,41 @@
     for partner in partners:
         pl.semaphore_signal(barrier, inc=1, device_id=partner, device_id_type=MESH)
 
+    def fetch(k, src, dst):
+        copy = pltpu.make_async_copy(src, dst, in_s.at[k])
+        copy.start()
+        return copy
+
+    cot_copy = fetch(0, cot_hbm, cot)
+    weight_copy = fetch(1, weight, wbuf.at[pl.ds(POS[0] * OWN, OWN)])
+    gate_copy = fetch(2, gate_hbm, gate)
+    up_copy = fetch(3, up_hbm, up)
+    cot_copy.wait()
     for p, r in enumerate(ORDER):
         start = pl.multiple_of(((y + r) % 4) * QD, 128)
         block = cot[:, pl.ds(start, QD)]
         for q in range(4):
             csrc[q, :, p * OWN : (p + 1) * OWN] = block[:, q * OWN : (q + 1) * OWN]
-    wbuf[pl.ds(POS[0] * OWN, OWN), :] = weight[...]
     cbuf[0, c, x] = csrc[xh * 2 + c]
 
     pl.semaphore_wait(barrier, len(partners))
 
     c_copies = {}
-    for i, (dx, dc) in enumerate(near):
-        nq = (((x + dx) % 4) // 2) * 2 + (c + dc) % 2
-        c_copies[dx, dc] = send(
-            csrc.at[nq], cbuf.at[0, c, x], c_s.at[i], c_r.at[i], at(dx=dx, dc=dc)
-        )
+
+    def send_c(*dxs):
+        for i, (dx, dc) in enumerate(near):
+            if dx in dxs:
+                nq = (((x + dx) % 4) // 2) * 2 + (c + dc) % 2
+                c_copies[dx, dc] = send(
+                    csrc.at[nq], cbuf.at[0, c, x], c_s.at[i], c_r.at[i], at(dx=dx, dc=dc)
+                )
+
+    send_c(0, 1, 3)
 
     def wrows(r, first=0, rows=OWN):
         return wbuf.at[pl.ds(POS[r] * OWN + first, rows)]
 
+    weight_copy.wait()
     w_up = send(wrows(0), wrows(3), w_s.at[0], w_r.at[0], at(dy=1))
     w_down = send(wrows(0), wrows(1), w_s.at[1], w_r.at[1], at(dy=3))
 
@@ -102,30 +118,55 @@
         hbuf[slot, c, pl.ds(xh * 2, 2)] = (activated * up_f32).astype(BF16)
         return 0
 
+    def send_z(way, k, src, dst):
+        to = at(dz=1 if way == 0 else 7)
+        return send(src, dst, z_s.at[way, k], z_r.at[way, k], to)
+
     def ring(step, j):
         xs = (x + SUBS[j]) % 4
         out = []
         for way in range(2):
-            if step == 3 and (j < 2) != (way == 0):
-                out.append(None)
-                continue
             src = 0 if step == 0 else 2 * step - 1 + way
-            dst = 7 if step == 3 else 2 * step + 1 + way
-            out.append(
-                send(
-                    cbuf.at[src, :, xs], cbuf.at[dst, :, xs],
-                    z_s.at[way, step, j], z_r.at[way, step, j],
-                    at(dz=1 if way == 0 else 7),
-                )
+            src, dst = cbuf.at[src, :, xs], cbuf.at[2 * step + 1 + way, :, xs]
+            out.append(send_z(way, 4 * step + j, src, dst))
+        return out
+
+    def ring_first(j):
+        xs, cols = (x + SUBS[j]) % 4, pl.ds(*CHUNKS[0])
+        return [
+            send_z(
+                way, 8 + j,
+                cbuf.at[3 + way, :, xs, :, cols], cbuf.at[5 + way, :, xs, :, cols],
             )
-        return out
+            for way in range(2)
+        ]
+
+    def ring_chunk(k):
+        cols = pl.ds(*CHUNKS[k])
+        return [
+            send_z(
+                way, 11 + k,
+                cbuf.at[3 + way, :, :, :, cols], cbuf.at[5 + way, :, :, :, cols],
+            )
+            for way in range(2)
+        ]
+
+    def ring_last(k, j=None):
+        cols = pl.ds(*CHUNKS[k])
+        xs = pl.ds(0, 4) if j is None else (x + SUBS[j]) % 4
+        sem = 14 + k if j is None else 18 + j
+        return [
+            send_z(
+                way, sem, cbuf.at[5 + way, way, xs, :, cols], cbuf.at[7, way, xs, :, cols]
+            )
+            for way in range(2)
+        ]
 
     ringed = {}
 
-    def arrive(step, j):
-        for copy in ringed[step, j]:
-            if copy is not None:
-                copy.wait_recv()
+    def arrive(*name):
+        for copy in ringed[name]:
+            copy.wait_recv()
 
     def forward(step):
         for j in range(4):
@@ -148,6 +189,8 @@
         h_copies["p", i].wait_recv()
         h_copies["f", i].wait_recv()
 
+    gate_copy.wait()
+    up_copy.wait()
     for j in range(4):
         lax.fori_loop(2 * j, 2 * j + 2, hidden, 0)
         dx = (4 - SUBS[j]) % 4
@@ -155,6 +198,8 @@
             if (dx, dc) != (0, 0):
                 c_copies[dx, dc].wait_recv()
         ringed[0, j] = ring(0, j)
+        if j == 2:
+            send_c(2)
     for i in range(4):
         send_h(i)
 
@@ -227,10 +272,10 @@
 
         lax.fori_loop(first, first + n, one, 0)
 
-    def partial_down(i, tile):
+    def partial_down(i, start, size):
         first, n = ROUNDS[i]
-        rows = pl.ds(pl.multiple_of(tile * TILE, TILE), TILE)
-        lhs = cbuf[pl.ds(first, n), :, :, :, rows].reshape(n * 256, TILE)
+        rows = pl.ds(start, size)
+        lhs = cbuf[pl.ds(first, n), :, :, :, rows].reshape(n * 256, size)
         for t in range(FF // TILE):
             cols = slice(t * TILE, (t + 1) * TILE)
             rhs = hbuf[pl.ds(first, n), :, :, :, cols].reshape(n * 256, TILE)
@@ -243,41 +288,37 @@
     def down_round(i):
         @pl.loop(0, QD // TILE)
         def _(tile):
-            partial_down(i, tile)
-
-    ringed[2, 0] = None
+            partial_down(i, pl.multiple_of(tile * TILE, TILE), TILE)
+
     for j in range(2):
         arrive(1, j)
-        ringed[2, j] = ring(2, j)
+        ringed["first", j] = ring_first(j)
     pass_h(1)
     arrive_h(0)
     arrive_h(1)
     down_round(0)
     for j in range(2, 4):
         arrive(1, j)
-        ringed[2, j] = ring(2, j)
+        ringed["first", j] = ring_first(j)
     w_up2.wait_recv()
     w_down2.wait_recv()
     partial_hidden(0)
+    pass_h(2)
+    for j in range(4):
+        arrive("first", j)
+        ringed["last", 0, j] = ring_last(0, j)
+    ringed["chunk", 1] = ring_chunk(1)
+    ringed["chunk", 2] = ring_chunk(2)
+    partial_hidden(1)
+    arrive_h(2)
+    pass_h(3)
     add_peer(0)
-    pass_h(2)
-    partial_hidden(1)
     add_peer(1)
-    for j in range(2):
-        arrive(2, j)
-        ringed[3, j] = ring(3, j)
-    arrive_h(2)
+    arrive("chunk", 1)
+    ringed["last", 1] = ring_last(1)
+    ringed["chunk", 3] = ring_chunk(3)
     down_round(1)
-    pass_h(3)
-    for j in range(2, 4):
-        arrive(2, j)
-        ringed[3, j] = ring(3, j)
-    partial_hidden(2)
-    add_peer(2)
     arrive_h(3)
-    down_round(2)
-    for j in range(4):
-        arrive(3, j)
 
     def gd_rows(r, first=0, rows=OWN):
         return pl.ds(POS[r] * OWN + first, rows)
@@ -291,30 +332,39 @@
         g[name] = send(gd_out.at[rows], dst, g_s.at[k], g_r.at[k], to)
 
     upward, downward = at(dy=1), at(dy=3)
-    partial_down(3, 0)
+    for j in range(4):
+        arrive("last", 0, j)
+    partial_down(2, *CHUNKS[0])
     round_gd(2)
     send_gd("u2", 0, gd_rows(2, 0, HALF), gd_half.at[0], upward)
     send_gd("d2", 1, gd_rows(2, HALF, HALF), gd_half.at[1], downward)
-    partial_down(3, 1)
+    arrive("chunk", 2)
+    ringed["last", 2] = ring_last(2)
+    arrive("last", 1)
+    partial_down(2, *CHUNKS[1])
     round_gd(1)
     send_gd("u1", 2, gd_rows(1, HALF, HALF), gd_in.at[0, pl.ds(HALF, HALF)], upward)
-    partial_down(3, 2)
+    arrive("chunk", 3)
+    ringed["last", 3] = ring_last(3)
+    arrive("last", 2)
+    partial_down(2, *CHUNKS[2])
     round_gd(3)
     send_gd("d1", 3, gd_rows(3, 0, HALF), gd_in.at[1, pl.ds(0, HALF)], downward)
-    partial_hidden(3)
-    add_peer(3)
-    finish_hidden(0)
     g["u2"].wait_recv()
     rows = gd_rows(1, 0, HALF)
     gd_out[rows] = (acc[rows, :] + gd_half[0].astype(F32)).astype(BF16)
     send_gd("u3", 4, rows, gd_in.at[0, pl.ds(0, HALF)], upward)
+    arrive("last", 3)
+    partial_hidden(2)
+    add_peer(2)
     g["d2"].wait_recv()
     rows = gd_rows(3, HALF, HALF)
     gd_out[rows] = (acc[rows, :] + gd_half[1].astype(F32)).astype(BF16)
     send_gd("d3", 5, rows, gd_in.at[1, pl.ds(HALF, HALF)], downward)
+    partial_down(2, *CHUNKS[3])
+    finish_hidden(0)
     finish_hidden(1)
     finish_hidden(2)
-    finish_hidden(3)
     g["u1"].wait_recv()
     g["d1"].wait_recv()
     g["u3"].wait_recv()
@@ -326,21 +376,31 @@
         copy.wait_send()
 
 
+def write_out(*refs):
+    copies = [
+        pltpu.make_async_copy(refs[i], refs[3 + i], refs[6].at[i]) for i in range(3)
+    ]
+    for copy in copies:
+        copy.start()
+    for copy in copies:
+        copy.wait()
+
+
 def on_device(gate_pre, up_saved, cotangent, down_weight):
     vmem = pl.BlockSpec(memory_space=pltpu.VMEM)
     dma = pltpu.SemaphoreType.DMA
     tokens = (2, 8, ROWS, FF)
-    grad_gate, grad_up, grad_down = pl.pallas_call(
+    shapes = (tokens, tokens, (OWN, FF))
+    results = pl.pallas_call(
         kernel,
         name="ffn_down_backward",
-        out_shape=(
-            jax.ShapeDtypeStruct(tokens, BF16),
-            jax.ShapeDtypeStruct(tokens, BF16),
-            jax.ShapeDtypeStruct((OWN, FF), BF16),
-        ),
-        in_specs=[vmem] * 4,
+        out_shape=tuple(pltpu.VMEM(shape, BF16) for shape in shapes),
+        in_specs=[pl.BlockSpec(memory_space=pl.ANY)] * 4,
         out_specs=(vmem,) * 3,
         scratch_shapes=[
+            pltpu.VMEM(tokens, BF16),
+            pltpu.VMEM(tokens, BF16),
+            pltpu.VMEM((ROWS, D), BF16),
             pltpu.VMEM((4, ROWS, QD), BF16),
             pltpu.VMEM((8, 2, 4, ROWS, QD), BF16),
             pltpu.VMEM((QD, FF), BF16),
@@ -356,16 +416,16 @@
             pltpu.VMEM((QD, FF), BF16),
             pltpu.VMEM((2, HALF, FF), BF16),
             pltpu.VMEM((2, OWN, FF), BF16),
-            dma((7,)), dma((7,)),
-            dma((2, 4, 4)), dma((2, 4, 4)),
+            dma((4,)), dma((7,)), dma((7,)),
+            dma((2, 22)), dma((2, 22)),
             dma((4,)), dma((4,)),
             dma((3, 4)), dma((3, 4)),
-            dma((4,)), dma((4,)),
-            dma((4,)), dma((4,)),
+            dma((3,)), dma((3,)),
+            dma((3,)), dma((3,)),
             dma((6,)), dma((6,)),
         ],
         compiler_params=pltpu.CompilerParams(
-            collective_id=0, has_side_effects=True, vmem_limit_bytes=60 << 20
+            collective_id=0, has_side_effects=True, vmem_limit_bytes=52 << 20
         ),
         cost_estimate=pl.CostEstimate(
             flops=4 * 2048 * QD * FF, bytes_accessed=7 << 20, transcendentals=512 * FF
@@ -373,6 +433,15 @@
     )(
         gate_pre.reshape(tokens), up_saved.reshape(tokens), cotangent, down_weight
     )
+    grad_gate, grad_up, grad_down = pl.pallas_call(
+        write_out,
+        name="write_out",
+        out_shape=tuple(jax.ShapeDtypeStruct(shape, BF16) for shape in shapes),
+        in_specs=[vmem] * 3,
+        out_specs=(pl.BlockSpec(memory_space=pl.ANY),) * 3,
+        scratch_shapes=[dma((3,))],
+        compiler_params=pltpu.CompilerParams(vmem_limit_bytes=8 << 20),
+    )(*[pltpu.with_memory_space_constraint(r, pltpu.VMEM) for r in results])
     return (grad_gate.reshape(512, FF), grad_up.reshape(512, FF), grad_down)
 
 

time: 95.9 us -> 86.7 us (0.904)
  local copies, waits for them, and re-layouts: 4.83 us -> 0 us
  Pallas kernels: 90.3 us -> 85.9 us
    unnamed x7 -> x0, local copies, waits for them, and re-layouts: 4.83 us -> none
    pallas_call x1 -> x2, Pallas kernels: 90.3 us -> 85.9 us  [the longest x1 84.3 us: on_device(): pl.pallas_call(kernel, name='ffn_down_backward', out_shape=tuple((pltpu.V...]
where the time goes in v2:
time: 86.7 us; the launch traced here: 86.6 us
  Pallas kernels  85.9 us (99%)
    pallas_call x1, Pallas kernels, on_device(): pl.pallas_call(kernel, name='ffn_down_backward', out_shape=tuple((pltpu.V...  84.3 us

profile of v2, /device:TPU:1, one launch (start us, length us, event | category | flops | bytes accessed | tf_op | source)
XLA Modules:
  0.0 86.6 jit_solution(15813660919894393852)
XLA Ops:
  0.6 84.3 %ffn_down_backward.1 = (bf16[2,8,32,1152]{3,2,1,0:T(8,128)(2,1)S(1)}, bf16[2,8,32,1152]{3,2,1,0:T(8,128)(2,1)S(1)}, bf16[288,1152]{1,0:T(8,128)(2,1)S(1)}) custom-call(bf16[2,8,32,1152]{3,2,1,0:T(8,128)(2,1)} %bitcast.4, bf16[2,8,32,1152]{3,2,1,0:T(8,128)(2,1)} %bitcast.5, bf16[32,4608]{1,0:T(8,128)(2,1)} %cot_hbm.1, bf16[288,1152]{1,0:T(8,128)(2,1)} %weight.1), custom_call_target="tpu_custom_call" | custom-call | flops 10871635968 | bytes 7340032 | tf_op jit(solution)/shard_map/ffn_down_backward/pallas_call | solution.py:394
  84.9 1.6 %write_out.1 = (bf16[2,8,32,1152]{3,2,1,0:T(8,128)(2,1)}, bf16[2,8,32,1152]{3,2,1,0:T(8,128)(2,1)}, bf16[288,1152]{1,0:T(8,128)(2,1)}) custom-call(bf16[2,8,32,1152]{3,2,1,0:T(8,128)(2,1)S(1)} %get-tuple-element.9.refs_0_, bf16[2,8,32,1152]{3,2,1,0:T(8,128)(2,1)S(1)} %get-tuple-element.10.refs_1_, bf16[288,1152]{1,0:T(8,128)(2,1)S(1)} %get-tuple-element.11.refs_2_), custom_call_target="tpu_custom_call" | custom-call | tf_op jit(solution)/shard_map/write_out/pallas_call | solution.py:436

commit v3 on v2

--- a/solution.py
+++ b/solution.py
@@ -20,10 +20,12 @@
 OWN = 288
 HALF = OWN // 2
 TILE = 384
-ORDER = (2, 1, 3, 0)
-POS = {r: p for p, r in enumerate(ORDER)}
+UNITS = ((2, 0), (2, 1), (1, 1), (3, 0), (1, 0), (3, 1), (0, 0), (0, 1))
+POS = {unit: k * HALF for k, unit in enumerate(UNITS)}
 SUBS = (0, 1, 3, 2)
-ROUNDS = ((0, 3), (3, 2), (5, 3))
+ROUNDS = ((0, 3), (3, 2), (5, 2), (7, 1))
+FAR = ((0, 1), (1, 2), (3, 2), (5, 2), (7, 1))
+DOWN = ((0, 3), (3, 2), (5, 3))
 CHUNKS = ((0, 384), (384, 256), (640, 256), (896, 256))
 
 
@@ -40,7 +42,7 @@
 def kernel(
     gate_hbm, up_hbm, cot_hbm, weight, grad_gate, grad_up, grad_down,
     gate, up, cot, csrc, cbuf, wbuf, hbuf, act, uder, acc,
-    peer_out, peer_in, kept, far_out, far_in, gd_out, gd_half, gd_in,
+    peer_out, peer_in, kept, theirs_acc, far_out, far_in, gd_out, gd_half, gd_in,
     in_s, c_s, c_r, z_s, z_r, w_s, w_r, h_s, h_r, p_s, p_r, f_s, f_r, g_s, g_r,
 ):
     dp, tensor = lax.axis_index("dp"), lax.axis_index("tensor")
@@ -74,15 +76,16 @@
         return copy
 
     cot_copy = fetch(0, cot_hbm, cot)
-    weight_copy = fetch(1, weight, wbuf.at[pl.ds(POS[0] * OWN, OWN)])
+    weight_copy = fetch(1, weight, wbuf.at[pl.ds(POS[0, 0], OWN)])
     gate_copy = fetch(2, gate_hbm, gate)
     up_copy = fetch(3, up_hbm, up)
     cot_copy.wait()
-    for p, r in enumerate(ORDER):
+    for (r, half), pos in POS.items():
         start = pl.multiple_of(((y + r) % 4) * QD, 128)
         block = cot[:, pl.ds(start, QD)]
         for q in range(4):
-            csrc[q, :, p * OWN : (p + 1) * OWN] = block[:, q * OWN : (q + 1) * OWN]
+            first = q * OWN + half * HALF
+            csrc[q, :, pos : pos + HALF] = block[:, first : first + HALF]
     cbuf[0, c, x] = csrc[xh * 2 + c]
 
     pl.semaphore_wait(barrier, len(partners))
@@ -99,12 +102,17 @@
 
     send_c(0, 1, 3)
 
-    def wrows(r, first=0, rows=OWN):
-        return wbuf.at[pl.ds(POS[r] * OWN + first, rows)]
-
+    def rows(r, half):
+        return pl.ds(POS[r, half], HALF)
+
+    def send_w(k, src, dst, to):
+        return send(wbuf.at[rows(*src)], wbuf.at[rows(*dst)], w_s.at[k], w_r.at[k], to)
+
+    upward, downward = at(dy=1), at(dy=3)
     weight_copy.wait()
-    w_up = send(wrows(0), wrows(3), w_s.at[0], w_r.at[0], at(dy=1))
-    w_down = send(wrows(0), wrows(1), w_s.at[1], w_r.at[1], at(dy=3))
+    w_up = send_w(0, (0, 0), (3, 0), upward)
+    w_down = send_w(1, (0, 1), (1, 1), downward)
+    w_rest = [send_w(2, (0, 1), (3, 1), upward), send_w(3, (0, 0), (1, 0), downward)]
 
     def z_of(slot):
         return (z + (1 - 2 * (slot % 2)) * ((slot + 1) // 2) + 8) % 8
@@ -191,8 +199,8 @@
 
     gate_copy.wait()
     up_copy.wait()
+    lax.fori_loop(0, 8, hidden, 0)
     for j in range(4):
-        lax.fori_loop(2 * j, 2 * j + 2, hidden, 0)
         dx = (4 - SUBS[j]) % 4
         for dc in range(2):
             if (dx, dc) != (0, 0):
@@ -200,43 +208,45 @@
         ringed[0, j] = ring(0, j)
         if j == 2:
             send_c(2)
-    for i in range(4):
-        send_h(i)
+            for i in range(4):
+                send_h(i)
 
     forward(1)
     w_up.wait_recv()
-    w_up2 = send(wrows(3, 0, HALF), wrows(2, 0, HALF), w_s.at[2], w_r.at[2], at(dy=1))
+    w_rest.append(send_w(4, (3, 0), (2, 0), upward))
     w_down.wait_recv()
-    w_down2 = send(
-        wrows(1, HALF, HALF), wrows(2, HALF, HALF), w_s.at[3], w_r.at[3], at(dy=3)
-    )
+    w_rest.append(send_w(5, (1, 1), (2, 1), downward))
     pass_h(0)
 
-    def grad_hidden(first, n, cp, store):
-        @pl.loop(0, FF // TILE)
-        def _(t):
-            cols = pl.ds(pl.multiple_of(t * TILE, TILE), TILE)
-            lhs = cbuf[pl.ds(first, n), cp].reshape(n * 128, QD)
-            out = jnp.dot(lhs, wbuf[:, cols], preferred_element_type=F32)
-            store(cols, out.reshape(n, 4, ROWS, TILE))
-
     p_copies, f_copies = {}, {}
 
-    def partial_hidden(i):
+    def partial_hidden(i, start=0, size=QD):
         first, n = ROUNDS[i]
-        slots = pl.ds(first, n)
-
-        def to_peer(cols, out):
-            peer_out[slots, :, :, cols] = out.astype(BF16)
-
-        def keep(cols, out):
-            kept[slots, :, :, cols] = out
-
-        grad_hidden(first, n, 1 - c, to_peer)
-        p_copies[i] = send(
-            peer_out.at[slots], peer_in.at[slots], p_s.at[i], p_r.at[i], at(dc=1)
-        )
-        grad_hidden(first, n, c, keep)
+        begin, end = start == 0, start + size == QD
+        cols = pl.ds(start, size)
+
+        def one(slot, _):
+            lhs = jnp.concatenate(
+                [cbuf[slot, cp, :, :, cols].reshape(128, size) for cp in (1 - c, c)]
+            )
+            out = jnp.dot(lhs, wbuf[cols, :], preferred_element_type=F32)
+            theirs, mine = out.reshape(2, 4, ROWS, FF)
+            if not begin:
+                theirs += theirs_acc[slot - 5]
+                mine += kept[slot]
+            kept[slot] = mine
+            if end:
+                peer_out[slot] = theirs.astype(BF16)
+            else:
+                theirs_acc[slot - 5] = theirs
+            return 0
+
+        lax.fori_loop(first, first + n, one, 0)
+        if end:
+            slots = pl.ds(first, n)
+            p_copies[i] = send(
+                peer_out.at[slots], peer_in.at[slots], p_s.at[i], p_r.at[i], at(dc=1)
+            )
 
     def add_peer(i):
         first, n = ROUNDS[i]
@@ -249,13 +259,15 @@
             return 0
 
         lax.fori_loop(first, first + n, one, 0)
-        slots = pl.ds(first, n)
+
+    def send_far(i):
+        slots = pl.ds(*FAR[i])
         f_copies[i] = send(
             far_out.at[slots], far_in.at[slots], f_s.at[i], f_r.at[i], at(dx=2)
         )
 
     def finish_hidden(i):
-        first, n = ROUNDS[i]
+        first, n = FAR[i]
         f_copies[i].wait_recv()
 
         def one(slot, _):
@@ -273,17 +285,15 @@
         lax.fori_loop(first, first + n, one, 0)
 
     def partial_down(i, start, size):
-        first, n = ROUNDS[i]
-        rows = pl.ds(start, size)
-        lhs = cbuf[pl.ds(first, n), :, :, :, rows].reshape(n * 256, size)
-        for t in range(FF // TILE):
-            cols = slice(t * TILE, (t + 1) * TILE)
-            rhs = hbuf[pl.ds(first, n), :, :, :, cols].reshape(n * 256, TILE)
-            out = lax.dot_general(lhs, rhs, (((0,), (0,)), ((), ())), preferred_element_type=F32)
-            if i == 0:
-                acc[rows, cols] = out
-            else:
-                acc[rows, cols] += out
+        first, n = DOWN[i]
+        cols = pl.ds(start, size)
+        lhs = cbuf[pl.ds(first, n), :, :, :, cols].reshape(n * 256, size)
+        rhs = hbuf[pl.ds(first, n)].reshape(n * 256, FF)
+        out = lax.dot_general(lhs, rhs, (((0,), (0,)), ((), ())), preferred_element_type=F32)
+        if i == 0:
+            acc[cols, :] = out
+        else:
+            acc[cols, :] += out
 
     def down_round(i):
         @pl.loop(0, QD // TILE)
@@ -300,8 +310,8 @@
     for j in range(2, 4):
         arrive(1, j)
         ringed["first", j] = ring_first(j)
-    w_up2.wait_recv()
-    w_down2.wait_recv()
+    for copy in w_rest:
+        copy.wait_recv()
     partial_hidden(0)
     pass_h(2)
     for j in range(4):
@@ -309,68 +319,68 @@
         ringed["last", 0, j] = ring_last(0, j)
     ringed["chunk", 1] = ring_chunk(1)
     ringed["chunk", 2] = ring_chunk(2)
+    add_peer(0)
     partial_hidden(1)
-    arrive_h(2)
     pass_h(3)
-    add_peer(0)
+    send_far(0)
+    send_far(1)
     add_peer(1)
+    send_far(2)
     arrive("chunk", 1)
     ringed["last", 1] = ring_last(1)
     ringed["chunk", 3] = ring_chunk(3)
+    arrive_h(2)
     down_round(1)
     arrive_h(3)
 
-    def gd_rows(r, first=0, rows=OWN):
-        return pl.ds(POS[r] * OWN + first, rows)
-
-    def round_gd(r):
-        gd_out[gd_rows(r)] = acc[gd_rows(r), :].astype(BF16)
-
-    g = {}
-
-    def send_gd(name, k, rows, dst, to):
-        g[name] = send(gd_out.at[rows], dst, g_s.at[k], g_r.at[k], to)
-
-    upward, downward = at(dy=1), at(dy=3)
+    def send_gd(k, src, dst, to, halves=None):
+        at_rows = rows(*src)
+        total = acc[at_rows, :]
+        if halves is not None:
+            total += halves[...].astype(F32)
+        gd_out[at_rows] = total.astype(BF16)
+        return send(gd_out.at[at_rows], dst, g_s.at[k], g_r.at[k], to)
+
+    def half_of(k, half):
+        return gd_in.at[k, pl.ds(half * HALF, HALF)]
+
     for j in range(4):
         arrive("last", 0, j)
     partial_down(2, *CHUNKS[0])
-    round_gd(2)
-    send_gd("u2", 0, gd_rows(2, 0, HALF), gd_half.at[0], upward)
-    send_gd("d2", 1, gd_rows(2, HALF, HALF), gd_half.at[1], downward)
+    up_far = send_gd(0, (2, 0), gd_half.at[0], upward)
+    down_far = send_gd(1, (2, 1), gd_half.at[1], downward)
     arrive("chunk", 2)
     ringed["last", 2] = ring_last(2)
+    partial_hidden(2, 0, CHUNKS[2][0])
     arrive("last", 1)
     partial_down(2, *CHUNKS[1])
-    round_gd(1)
-    send_gd("u1", 2, gd_rows(1, HALF, HALF), gd_in.at[0, pl.ds(HALF, HALF)], upward)
+    arrivals = [
+        send_gd(2, (1, 1), half_of(0, 1), upward),
+        send_gd(3, (3, 0), half_of(1, 0), downward),
+    ]
     arrive("chunk", 3)
     ringed["last", 3] = ring_last(3)
+    partial_hidden(2, CHUNKS[2][0], QD - CHUNKS[2][0])
     arrive("last", 2)
     partial_down(2, *CHUNKS[2])
-    round_gd(3)
-    send_gd("d1", 3, gd_rows(3, 0, HALF), gd_in.at[1, pl.ds(0, HALF)], downward)
-    g["u2"].wait_recv()
-    rows = gd_rows(1, 0, HALF)
-    gd_out[rows] = (acc[rows, :] + gd_half[0].astype(F32)).astype(BF16)
-    send_gd("u3", 4, rows, gd_in.at[0, pl.ds(0, HALF)], upward)
+    add_peer(2)
+    send_far(3)
+    up_far.wait_recv()
+    arrivals.append(send_gd(4, (1, 0), half_of(0, 0), upward, gd_half.at[0]))
+    down_far.wait_recv()
+    arrivals.append(send_gd(5, (3, 1), half_of(1, 1), downward, gd_half.at[1]))
+    partial_hidden(3, 0, CHUNKS[3][0])
     arrive("last", 3)
-    partial_hidden(2)
-    add_peer(2)
-    g["d2"].wait_recv()
-    rows = gd_rows(3, HALF, HALF)
-    gd_out[rows] = (acc[rows, :] + gd_half[1].astype(F32)).astype(BF16)
-    send_gd("d3", 5, rows, gd_in.at[1, pl.ds(HALF, HALF)], downward)
+    partial_hidden(3, *CHUNKS[3])
     partial_down(2, *CHUNKS[3])
-    finish_hidden(0)
-    finish_hidden(1)
-    finish_hidden(2)
-    g["u1"].wait_recv()
-    g["d1"].wait_recv()
-    g["u3"].wait_recv()
-    g["d3"].wait_recv()
+    add_peer(3)
+    send_far(4)
+    for i in range(5):
+        finish_hidden(i)
+    for copy in arrivals:
+        copy.wait_recv()
     grad_down[...] = (
-        acc[gd_rows(0), :] + gd_in[0].astype(F32) + gd_in[1].astype(F32)
+        acc[pl.ds(POS[0, 0], OWN), :] + gd_in[0].astype(F32) + gd_in[1].astype(F32)
     ).astype(BF16)
     for copy in started:
         copy.wait_send()
@@ -411,6 +421,7 @@
             pltpu.VMEM((8, 4, ROWS, FF), BF16),
             pltpu.VMEM((8, 4, ROWS, FF), BF16),
             pltpu.VMEM((8, 4, ROWS, FF), F32),
+            pltpu.VMEM((3, 4, ROWS, FF), F32),
             pltpu.VMEM((8, 2, ROWS, FF), BF16),
             pltpu.VMEM((8, 2, ROWS, FF), BF16),
             pltpu.VMEM((QD, FF), BF16),
@@ -418,10 +429,10 @@
             pltpu.VMEM((2, OWN, FF), BF16),
             dma((4,)), dma((7,)), dma((7,)),
             dma((2, 22)), dma((2, 22)),
+            dma((6,)), dma((6,)),
+            dma((3, 4)), dma((3, 4)),
             dma((4,)), dma((4,)),
-            dma((3, 4)), dma((3, 4)),
-            dma((3,)), dma((3,)),
-            dma((3,)), dma((3,)),
+            dma((5,)), dma((5,)),
             dma((6,)), dma((6,)),
         ],
         compiler_params=pltpu.CompilerParams(

time: 86.7 us -> 78.9 us (0.910)
  Pallas kernels: 85.9 us -> 77.9 us
    pallas_call x1, Pallas kernels: 84.3 us -> 76.3 us  [on_device(): pl.pallas_call(kernel, name='ffn_down_backward', out_shape=tuple((pltpu.V...]
where the time goes in v3:
time: 78.9 us; the launch traced here: 78.5 us
  Pallas kernels  77.9 us (99%)
    pallas_call x1, Pallas kernels, on_device(): pl.pallas_call(kernel, name='ffn_down_backward', out_shape=tuple((pltpu.V...  76.3 us
    pallas_call x1, Pallas kernels, on_device(): pl.pallas_call(write_out, name='write_out', out_shape=tuple((jax.ShapeDty...  1.64 us

profile of v3, /device:TPU:1, one launch (start us, length us, event | category | flops | bytes accessed | tf_op | source)
XLA Modules:
  0.0 78.5 jit_solution(18300901212113721257)
XLA Ops:
  0.6 76.3 %ffn_down_backward.1 = (bf16[2,8,32,1152]{3,2,1,0:T(8,128)(2,1)S(1)}, bf16[2,8,32,1152]{3,2,1,0:T(8,128)(2,1)S(1)}, bf16[288,1152]{1,0:T(8,128)(2,1)S(1)}) custom-call(bf16[2,8,32,1152]{3,2,1,0:T(8,128)(2,1)} %bitcast.4, bf16[2,8,32,1152]{3,2,1,0:T(8,128)(2,1)} %bitcast.5, bf16[32,4608]{1,0:T(8,128)(2,1)} %cot_hbm.1, bf16[288,1152]{1,0:T(8,128)(2,1)} %weight.1), custom_call_target="tpu_custom_call" | custom-call | flops 10871635968 | bytes 7340032 | tf_op jit(solution)/shard_map/ffn_down_backward/pallas_call | solution.py:404
  76.9 1.6 %write_out.1 = (bf16[2,8,32,1152]{3,2,1,0:T(8,128)(2,1)}, bf16[2,8,32,1152]{3,2,1,0:T(8,128)(2,1)}, bf16[288,1152]{1,0:T(8,128)(2,1)}) custom-call(bf16[2,8,32,1152]{3,2,1,0:T(8,128)(2,1)S(1)} %get-tuple-element.9.refs_0_, bf16[2,8,32,1152]{3,2,1,0:T(8,128)(2,1)S(1)} %get-tuple-element.10.refs_1_, bf16[288,1152]{1,0:T(8,128)(2,1)S(1)} %get-tuple-element.11.refs_2_), custom_call_target="tpu_custom_call" | custom-call | tf_op jit(solution)/shard_map/write_out/pallas_call | solution.py:447

commit v4 on v3

--- a/solution.py
+++ b/solution.py
@@ -24,9 +24,9 @@
 POS = {unit: k * HALF for k, unit in enumerate(UNITS)}
 SUBS = (0, 1, 3, 2)
 ROUNDS = ((0, 3), (3, 2), (5, 2), (7, 1))
-FAR = ((0, 1), (1, 2), (3, 2), (5, 2), (7, 1))
-DOWN = ((0, 3), (3, 2), (5, 3))
+LATE = (3, 5)
 CHUNKS = ((0, 384), (384, 256), (640, 256), (896, 256))
+PARTS = ((0, 512), (512, 640))
 
 
 def gelu_parts(gate_f32):
@@ -130,67 +130,50 @@
         to = at(dz=1 if way == 0 else 7)
         return send(src, dst, z_s.at[way, k], z_r.at[way, k], to)
 
-    def ring(step, j):
+    def ring(j):
         xs = (x + SUBS[j]) % 4
+        ringed[0, 0, j] = [
+            send_z(way, j, cbuf.at[0, :, xs], cbuf.at[1 + way, :, xs]) for way in range(2)
+        ]
+
+    counter = [4]
+
+    def ring_chunk(level, k, j=None):
+        cols = pl.ds(*CHUNKS[k])
+        xs = pl.ds(0, 4) if j is None else (x + SUBS[j]) % 4
         out = []
         for way in range(2):
-            src = 0 if step == 0 else 2 * step - 1 + way
-            src, dst = cbuf.at[src, :, xs], cbuf.at[2 * step + 1 + way, :, xs]
-            out.append(send_z(way, 4 * step + j, src, dst))
-        return out
-
-    def ring_first(j):
-        xs, cols = (x + SUBS[j]) % 4, pl.ds(*CHUNKS[0])
-        return [
-            send_z(
-                way, 8 + j,
-                cbuf.at[3 + way, :, xs, :, cols], cbuf.at[5 + way, :, xs, :, cols],
+            src, dst = 2 * level - 1 + way, 7 if level == 3 else 2 * level + 1 + way
+            core = way if level == 3 else pl.ds(0, 2)
+            out.append(
+                send_z(
+                    way, counter[0],
+                    cbuf.at[src, core, xs, :, cols], cbuf.at[dst, core, xs, :, cols],
+                )
             )
-            for way in range(2)
-        ]
-
-    def ring_chunk(k):
-        cols = pl.ds(*CHUNKS[k])
-        return [
-            send_z(
-                way, 11 + k,
-                cbuf.at[3 + way, :, :, :, cols], cbuf.at[5 + way, :, :, :, cols],
-            )
-            for way in range(2)
-        ]
-
-    def ring_last(k, j=None):
-        cols = pl.ds(*CHUNKS[k])
-        xs = pl.ds(0, 4) if j is None else (x + SUBS[j]) % 4
-        sem = 14 + k if j is None else 18 + j
-        return [
-            send_z(
-                way, sem, cbuf.at[5 + way, way, xs, :, cols], cbuf.at[7, way, xs, :, cols]
-            )
-            for way in range(2)
-        ]
+        counter[0] += 1
+        ringed[level, k, j] = out
 
     ringed = {}
 
-    def arrive(*name):
-        for copy in ringed[name]:
+    def arrive(level, k, j=None):
+        for copy in ringed[level, k, j]:
             copy.wait_recv()
 
-    def forward(step):
-        for j in range(4):
-            arrive(step - 1, j)
-            ringed[step, j] = ring(step, j)
-
     h_copies = {}
 
+    def hidden_piece(i, from_xh):
+        slots, cols = pl.ds(4 * (i % 2), 4), pl.ds(*PARTS[i // 2])
+        return hbuf.at[slots, c, pl.ds(from_xh * 2, 2), :, cols]
+
     def send_h(i):
-        mine = hbuf.at[pl.ds(2 * i, 2), c, pl.ds(xh * 2, 2)]
+        mine = hidden_piece(i, xh)
         h_copies["p", i] = send(mine, mine, h_s.at[0, i], h_r.at[0, i], at(dc=1))
         h_copies["x", i] = send(mine, mine, h_s.at[1, i], h_r.at[1, i], at(dx=2))
 
     def pass_h(i):
         h_copies["x", i].wait_recv()
-        theirs = hbuf.at[pl.ds(2 * i, 2), c, pl.ds((1 - xh) * 2, 2)]
+        theirs = hidden_piece(i, 1 - xh)
         h_copies["f", i] = send(theirs, theirs, h_s.at[2, i], h_r.at[2, i], at(dc=1))
 
     def arrive_h(i):
@@ -205,18 +188,11 @@
         for dc in range(2):
             if (dx, dc) != (0, 0):
                 c_copies[dx, dc].wait_recv()
-        ringed[0, j] = ring(0, j)
+        ring(j)
         if j == 2:
             send_c(2)
             for i in range(4):
                 send_h(i)
-
-    forward(1)
-    w_up.wait_recv()
-    w_rest.append(send_w(4, (3, 0), (2, 0), upward))
-    w_down.wait_recv()
-    w_rest.append(send_w(5, (1, 1), (2, 1), downward))
-    pass_h(0)
 
     p_copies, f_copies = {}, {}
 
@@ -232,13 +208,13 @@
             out = jnp.dot(lhs, wbuf[cols, :], preferred_element_type=F32)
             theirs, mine = out.reshape(2, 4, ROWS, FF)
             if not begin:
-                theirs += theirs_acc[slot - 5]
+                theirs += theirs_acc[slot - LATE[0]]
                 mine += kept[slot]
             kept[slot] = mine
             if end:
                 peer_out[slot] = theirs.astype(BF16)
             else:
-                theirs_acc[slot - 5] = theirs
+                theirs_acc[slot - LATE[0]] = theirs
             return 0
 
         lax.fori_loop(first, first + n, one, 0)
@@ -261,13 +237,13 @@
         lax.fori_loop(first, first + n, one, 0)
 
     def send_far(i):
-        slots = pl.ds(*FAR[i])
+        slots = pl.ds(*ROUNDS[i])
         f_copies[i] = send(
             far_out.at[slots], far_in.at[slots], f_s.at[i], f_r.at[i], at(dx=2)
         )
 
     def finish_hidden(i):
-        first, n = FAR[i]
+        first, n = ROUNDS[i]
         f_copies[i].wait_recv()
 
         def one(slot, _):
@@ -284,101 +260,135 @@
 
         lax.fori_loop(first, first + n, one, 0)
 
-    def partial_down(i, start, size):
-        first, n = DOWN[i]
-        cols = pl.ds(start, size)
+    def partial_down(first, n, start, size, part):
+        cols, units = pl.ds(start, size), pl.ds(*PARTS[part])
         lhs = cbuf[pl.ds(first, n), :, :, :, cols].reshape(n * 256, size)
-        rhs = hbuf[pl.ds(first, n)].reshape(n * 256, FF)
+        rhs = hbuf[pl.ds(first, n), :, :, :, units].reshape(n * 256, PARTS[part][1])
         out = lax.dot_general(lhs, rhs, (((0,), (0,)), ((), ())), preferred_element_type=F32)
-        if i == 0:
-            acc[cols, :] = out
+        if first == 0:
+            acc[cols, units] = out
         else:
-            acc[cols, :] += out
-
-    def down_round(i):
+            acc[cols, units] += out
+
+    def early_down(part):
         @pl.loop(0, QD // TILE)
         def _(tile):
-            partial_down(i, pl.multiple_of(tile * TILE, TILE), TILE)
-
-    for j in range(2):
-        arrive(1, j)
-        ringed["first", j] = ring_first(j)
+            partial_down(*ROUNDS[0], pl.multiple_of(tile * TILE, TILE), TILE, part)
+
+    def late_down(k, part):
+        partial_down(*LATE, *CHUNKS[k], part)
+
+    gd = {}
+
+    def send_gd(unit, part, way, dst, halves=None):
+        at_rows, units = rows(*unit), pl.ds(*PARTS[part])
+        total = acc[at_rows, units]
+        if halves is not None:
+            total += halves[:, units].astype(F32)
+        gd_out[at_rows, units] = total.astype(BF16)
+        k = len(gd)
+        gd[unit, part] = send(
+            gd_out.at[at_rows, units], dst.at[:, units],
+            g_s.at[k], g_r.at[k], (upward, downward)[way],
+        )
+
+    def half_of(k, half):
+        return gd_in.at[k, pl.ds(half * HALF, HALF)]
+
+    def send_two(part):
+        send_gd((2, 0), part, 0, gd_half.at[0])
+        send_gd((2, 1), part, 1, gd_half.at[1])
+
+    def send_one(part):
+        send_gd((1, 1), part, 0, half_of(0, 1))
+        send_gd((3, 0), part, 1, half_of(1, 0))
+
+    def send_rest(part):
+        gd[(2, 0), part].wait_recv()
+        send_gd((1, 0), part, 0, half_of(0, 0), gd_half.at[0])
+        gd[(2, 1), part].wait_recv()
+        send_gd((3, 1), part, 1, half_of(1, 1), gd_half.at[1])
+
+    for j in range(4):
+        arrive(0, 0, j)
+        ring_chunk(1, 0, j)
+        if j == 2:
+            w_up.wait_recv()
+            w_rest.append(send_w(4, (3, 0), (2, 0), upward))
+            w_down.wait_recv()
+            w_rest.append(send_w(5, (1, 1), (2, 1), downward))
+    pass_h(0)
+    for j in range(4):
+        arrive(1, 0, j)
+        ring_chunk(2, 0, j)
+    ring_chunk(1, 1)
+    arrive_h(0)
+    early_down(0)
     pass_h(1)
-    arrive_h(0)
-    arrive_h(1)
-    down_round(0)
-    for j in range(2, 4):
-        arrive(1, j)
-        ringed["first", j] = ring_first(j)
+    for j in range(4):
+        arrive(2, 0, j)
+        ring_chunk(3, 0, j)
     for copy in w_rest:
         copy.wait_recv()
     partial_hidden(0)
+    arrive(1, 1)
+    ring_chunk(2, 1)
+    ring_chunk(1, 2)
     pass_h(2)
+    add_peer(0)
+    send_far(0)
+    arrive_h(1)
     for j in range(4):
-        arrive("first", j)
-        ringed["last", 0, j] = ring_last(0, j)
-    ringed["chunk", 1] = ring_chunk(1)
-    ringed["chunk", 2] = ring_chunk(2)
-    add_peer(0)
-    partial_hidden(1)
+        arrive(3, 0, j)
+    late_down(0, 0)
+    send_two(0)
+    partial_hidden(1, 0, CHUNKS[2][0])
+    arrive(2, 1)
+    ring_chunk(3, 1)
+    ring_chunk(1, 3)
+    arrive_h(2)
+    early_down(1)
     pass_h(3)
-    send_far(0)
+    arrive(1, 2)
+    ring_chunk(2, 2)
+    arrive(3, 1)
+    late_down(1, 0)
+    send_one(0)
+    arrive_h(3)
+    late_down(0, 1)
+    send_two(1)
+    late_down(1, 1)
+    send_one(1)
+    arrive(1, 3)
+    ring_chunk(2, 3)
+    partial_hidden(1, CHUNKS[2][0], QD - CHUNKS[2][0])
+    arrive(2, 2)
+    ring_chunk(3, 2)
+    add_peer(1)
     send_far(1)
-    add_peer(1)
+    partial_hidden(2, 0, CHUNKS[2][0])
+    partial_hidden(3, 0, CHUNKS[2][0])
+    arrive(2, 3)
+    ring_chunk(3, 3)
+    partial_hidden(2, CHUNKS[2][0], QD - CHUNKS[2][0])
+    arrive(3, 2)
+    late_down(2, 0)
+    send_rest(0)
+    late_down(2, 1)
+    send_rest(1)
+    add_peer(2)
     send_far(2)
-    arrive("chunk", 1)
-    ringed["last", 1] = ring_last(1)
-    ringed["chunk", 3] = ring_chunk(3)
-    arrive_h(2)
-    down_round(1)
-    arrive_h(3)
-
-    def send_gd(k, src, dst, to, halves=None):
-        at_rows = rows(*src)
-        total = acc[at_rows, :]
-        if halves is not None:
-            total += halves[...].astype(F32)
-        gd_out[at_rows] = total.astype(BF16)
-        return send(gd_out.at[at_rows], dst, g_s.at[k], g_r.at[k], to)
-
-    def half_of(k, half):
-        return gd_in.at[k, pl.ds(half * HALF, HALF)]
-
-    for j in range(4):
-        arrive("last", 0, j)
-    partial_down(2, *CHUNKS[0])
-    up_far = send_gd(0, (2, 0), gd_half.at[0], upward)
-    down_far = send_gd(1, (2, 1), gd_half.at[1], downward)
-    arrive("chunk", 2)
-    ringed["last", 2] = ring_last(2)
-    partial_hidden(2, 0, CHUNKS[2][0])
-    arrive("last", 1)
-    partial_down(2, *CHUNKS[1])
-    arrivals = [
-        send_gd(2, (1, 1), half_of(0, 1), upward),
-        send_gd(3, (3, 0), half_of(1, 0), downward),
-    ]
-    arrive("chunk", 3)
-    ringed["last", 3] = ring_last(3)
-    partial_hidden(2, CHUNKS[2][0], QD - CHUNKS[2][0])
-    arrive("last", 2)
-    partial_down(2, *CHUNKS[2])
-    add_peer(2)
+    arrive(3, 3)
+    partial_hidden(3, CHUNKS[2][0], QD - CHUNKS[2][0])
+    late_down(3, 0)
+    late_down(3, 1)
+    add_peer(3)
     send_far(3)
-    up_far.wait_recv()
-    arrivals.append(send_gd(4, (1, 0), half_of(0, 0), upward, gd_half.at[0]))
-    down_far.wait_recv()
-    arrivals.append(send_gd(5, (3, 1), half_of(1, 1), downward, gd_half.at[1]))
-    partial_hidden(3, 0, CHUNKS[3][0])
-    arrive("last", 3)
-    partial_hidden(3, *CHUNKS[3])
-    partial_down(2, *CHUNKS[3])
-    add_peer(3)
-    send_far(4)
-    for i in range(5):
+    for i in range(4):
         finish_hidden(i)
-    for copy in arrivals:
-        copy.wait_recv()
+    for part in range(2):
+        for unit in ((1, 0), (1, 1), (3, 0), (3, 1)):
+            gd[unit, part].wait_recv()
     grad_down[...] = (
         acc[pl.ds(POS[0, 0], OWN), :] + gd_in[0].astype(F32) + gd_in[1].astype(F32)
     ).astype(BF16)
@@ -421,19 +431,19 @@
             pltpu.VMEM((8, 4, ROWS, FF), BF16),
             pltpu.VMEM((8, 4, ROWS, FF), BF16),
             pltpu.VMEM((8, 4, ROWS, FF), F32),
-            pltpu.VMEM((3, 4, ROWS, FF), F32),
+            pltpu.VMEM((LATE[1], 4, ROWS, FF), F32),
             pltpu.VMEM((8, 2, ROWS, FF), BF16),
             pltpu.VMEM((8, 2, ROWS, FF), BF16),
             pltpu.VMEM((QD, FF), BF16),
             pltpu.VMEM((2, HALF, FF), BF16),
             pltpu.VMEM((2, OWN, FF), BF16),
             dma((4,)), dma((7,)), dma((7,)),
-            dma((2, 22)), dma((2, 22)),
+            dma((2, 25)), dma((2, 25)),
             dma((6,)), dma((6,)),
             dma((3, 4)), dma((3, 4)),
             dma((4,)), dma((4,)),
-            dma((5,)), dma((5,)),
-            dma((6,)), dma((6,)),
+            dma((4,)), dma((4,)),
+            dma((12,)), dma((12,)),
         ],
         compiler_params=pltpu.CompilerParams(
             collective_id=0, has_side_effects=True, vmem_limit_bytes=52 << 20

time: 78.9 us -> 76.5 us (0.970)
  Pallas kernels: 77.9 us -> 75.8 us
    pallas_call x1, Pallas kernels: 76.3 us -> 74.2 us  [on_device(): pl.pallas_call(kernel, name='ffn_down_backward', out_shape=tuple((pltpu.V...]
where the time goes in v4:
time: 76.5 us; the launch traced here: 76.4 us
  Pallas kernels  75.8 us (99%)
    pallas_call x1, Pallas kernels, on_device(): pl.pallas_call(kernel, name='ffn_down_backward', out_shape=tuple((pltpu.V...  74.2 us
    pallas_call x1, Pallas kernels, on_device(): pl.pallas_call(write_out, name='write_out', out_shape=tuple((jax.ShapeDty...  1.64 us

profile of v4, /device:TPU:1, one launch (start us, length us, event | category | flops | bytes accessed | tf_op | source)
XLA Modules:
  0.0 76.4 jit_solution(994276729084594387)
XLA Ops:
  0.6 74.2 %ffn_down_backward.1 = (bf16[2,8,32,1152]{3,2,1,0:T(8,128)(2,1)S(1)}, bf16[2,8,32,1152]{3,2,1,0:T(8,128)(2,1)S(1)}, bf16[288,1152]{1,0:T(8,128)(2,1)S(1)}) custom-call(bf16[2,8,32,1152]{3,2,1,0:T(8,128)(2,1)} %bitcast.4, bf16[2,8,32,1152]{3,2,1,0:T(8,128)(2,1)} %bitcast.5, bf16[32,4608]{1,0:T(8,128)(2,1)} %cot_hbm.1, bf16[288,1152]{1,0:T(8,128)(2,1)} %weight.1), custom_call_target="tpu_custom_call" | custom-call | flops 10871635968 | bytes 7340032 | tf_op jit(solution)/shard_map/ffn_down_backward/pallas_call | solution.py:414
  74.8 1.6 %write_out.1 = (bf16[2,8,32,1152]{3,2,1,0:T(8,128)(2,1)}, bf16[2,8,32,1152]{3,2,1,0:T(8,128)(2,1)}, bf16[288,1152]{1,0:T(8,128)(2,1)}) custom-call(bf16[2,8,32,1152]{3,2,1,0:T(8,128)(2,1)S(1)} %get-tuple-element.9.refs_0_, bf16[2,8,32,1152]{3,2,1,0:T(8,128)(2,1)S(1)} %get-tuple-element.10.refs_1_, bf16[288,1152]{1,0:T(8,128)(2,1)S(1)} %get-tuple-element.11.refs_2_), custom_call_target="tpu_custom_call" | custom-call | tf_op jit(solution)/shard_map/write_out/pallas_call | solution.py:457

commit v5 on v4

--- a/solution.py
+++ b/solution.py
@@ -344,47 +344,49 @@
     send_two(0)
     partial_hidden(1, 0, CHUNKS[2][0])
     arrive(2, 1)
+    ring_chunk(1, 3)
     ring_chunk(3, 1)
-    ring_chunk(1, 3)
     arrive_h(2)
     early_down(1)
     pass_h(3)
     arrive(1, 2)
     ring_chunk(2, 2)
-    arrive(3, 1)
-    late_down(1, 0)
-    send_one(0)
+    partial_hidden(1, *CHUNKS[2])
     arrive_h(3)
     late_down(0, 1)
     send_two(1)
+    arrive(1, 3)
+    ring_chunk(2, 3)
+    partial_hidden(1, *CHUNKS[3])
+    arrive(3, 1)
+    late_down(1, 0)
+    add_peer(1)
+    send_far(1)
+    send_one(0)
     late_down(1, 1)
     send_one(1)
-    arrive(1, 3)
-    ring_chunk(2, 3)
-    partial_hidden(1, CHUNKS[2][0], QD - CHUNKS[2][0])
+    partial_hidden(2, 0, CHUNKS[2][0])
     arrive(2, 2)
     ring_chunk(3, 2)
-    add_peer(1)
-    send_far(1)
-    partial_hidden(2, 0, CHUNKS[2][0])
+    partial_hidden(2, *CHUNKS[2])
     partial_hidden(3, 0, CHUNKS[2][0])
     arrive(2, 3)
     ring_chunk(3, 3)
-    partial_hidden(2, CHUNKS[2][0], QD - CHUNKS[2][0])
+    partial_hidden(2, *CHUNKS[3])
+    add_peer(2)
+    send_far(2)
     arrive(3, 2)
     late_down(2, 0)
     send_rest(0)
     late_down(2, 1)
     send_rest(1)
-    add_peer(2)
-    send_far(2)
     arrive(3, 3)
     partial_hidden(3, CHUNKS[2][0], QD - CHUNKS[2][0])
     late_down(3, 0)
-    late_down(3, 1)
     add_peer(3)
     send_far(3)
-    for i in range(4):
+    late_down(3, 1)
+    for i in range(3):
         finish_hidden(i)
     for part in range(2):
         for unit in ((1, 0), (1, 1), (3, 0), (3, 1)):
@@ -392,6 +394,7 @@
     grad_down[...] = (
         acc[pl.ds(POS[0, 0], OWN), :] + gd_in[0].astype(F32) + gd_in[1].astype(F32)
     ).astype(BF16)
+    finish_hidden(3)
     for copy in started:
         copy.wait_send()
 

time: 76.5 us -> 75.1 us (0.982)
  Pallas kernels: 75.8 us -> 74.4 us
    pallas_call x1, Pallas kernels: 74.2 us -> 72.8 us  [on_device(): pl.pallas_call(kernel, name='ffn_down_backward', out_shape=tuple((pltpu.V...]
where the time goes in v5:
time: 75.1 us; the launch traced here: 75 us
  Pallas kernels  74.4 us (99%)
    pallas_call x1, Pallas kernels, on_device(): pl.pallas_call(kernel, name='ffn_down_backward', out_shape=tuple((pltpu.V...  72.8 us
    pallas_call x1, Pallas kernels, on_device(): pl.pallas_call(write_out, name='write_out', out_shape=tuple((jax.ShapeDty...  1.64 us

profile of v5, /device:TPU:1, one launch (start us, length us, event | category | flops | bytes accessed | tf_op | source)
XLA Modules:
  0.0 75.0 jit_solution(3014139152464020817)
XLA Ops:
  0.6 72.8 %ffn_down_backward.1 = (bf16[2,8,32,1152]{3,2,1,0:T(8,128)(2,1)S(1)}, bf16[2,8,32,1152]{3,2,1,0:T(8,128)(2,1)S(1)}, bf16[288,1152]{1,0:T(8,128)(2,1)S(1)}) custom-call(bf16[2,8,32,1152]{3,2,1,0:T(8,128)(2,1)} %bitcast.4, bf16[2,8,32,1152]{3,2,1,0:T(8,128)(2,1)} %bitcast.5, bf16[32,4608]{1,0:T(8,128)(2,1)} %cot_hbm.1, bf16[288,1152]{1,0:T(8,128)(2,1)} %weight.1), custom_call_target="tpu_custom_call" | custom-call | flops 10871635968 | bytes 7340032 | tf_op jit(solution)/shard_map/ffn_down_backward/pallas_call | solution.py:417
  73.4 1.6 %write_out.1 = (bf16[2,8,32,1152]{3,2,1,0:T(8,128)(2,1)}, bf16[2,8,32,1152]{3,2,1,0:T(8,128)(2,1)}, bf16[288,1152]{1,0:T(8,128)(2,1)}) custom-call(bf16[2,8,32,1152]{3,2,1,0:T(8,128)(2,1)S(1)} %get-tuple-element.9.refs_0_, bf16[2,8,32,1152]{3,2,1,0:T(8,128)(2,1)S(1)} %get-tuple-element.10.refs_1_, bf16[288,1152]{1,0:T(8,128)(2,1)S(1)} %get-tuple-element.11.refs_2_), custom_call_target="tpu_custom_call" | custom-call | tf_op jit(solution)/shard_map/write_out/pallas_call | solution.py:460

commit v6 on v5

--- a/solution.py
+++ b/solution.py
@@ -180,15 +180,16 @@
         h_copies["p", i].wait_recv()
         h_copies["f", i].wait_recv()
 
-    gate_copy.wait()
-    up_copy.wait()
-    lax.fori_loop(0, 8, hidden, 0)
     for j in range(4):
         dx = (4 - SUBS[j]) % 4
         for dc in range(2):
             if (dx, dc) != (0, 0):
                 c_copies[dx, dc].wait_recv()
         ring(j)
+        if j == 0:
+            gate_copy.wait()
+            up_copy.wait()
+            lax.fori_loop(0, 8, hidden, 0)
         if j == 2:
             send_c(2)
             for i in range(4):
@@ -358,10 +359,10 @@
     arrive(1, 3)
     ring_chunk(2, 3)
     partial_hidden(1, *CHUNKS[3])
+    add_peer(1)
+    send_far(1)
     arrive(3, 1)
     late_down(1, 0)
-    add_peer(1)
-    send_far(1)
     send_one(0)
     late_down(1, 1)
     send_one(1)

time: 75.1 us -> 73.7 us (0.981)
  Pallas kernels: 74.4 us -> 73 us
    pallas_call x1, Pallas kernels: 72.8 us -> 71.3 us  [on_device(): pl.pallas_call(kernel, name='ffn_down_backward', out_shape=tuple((pltpu.V...]
where the time goes in v6:
time: 73.7 us; the launch traced here: 73.6 us
  Pallas kernels  73 us (99%)
    pallas_call x1, Pallas kernels, on_device(): pl.pallas_call(kernel, name='ffn_down_backward', out_shape=tuple((pltpu.V...  71.3 us
    pallas_call x1, Pallas kernels, on_device(): pl.pallas_call(write_out, name='write_out', out_shape=tuple((jax.ShapeDty...  1.64 us

profile of v6, /device:TPU:1, one launch (start us, length us, event | category | flops | bytes accessed | tf_op | source)
XLA Modules:
  0.0 73.6 jit_solution(8917750215137390692)
XLA Ops:
  0.6 71.3 %ffn_down_backward.1 = (bf16[2,8,32,1152]{3,2,1,0:T(8,128)(2,1)S(1)}, bf16[2,8,32,1152]{3,2,1,0:T(8,128)(2,1)S(1)}, bf16[288,1152]{1,0:T(8,128)(2,1)S(1)}) custom-call(bf16[2,8,32,1152]{3,2,1,0:T(8,128)(2,1)} %bitcast.4, bf16[2,8,32,1152]{3,2,1,0:T(8,128)(2,1)} %bitcast.5, bf16[32,4608]{1,0:T(8,128)(2,1)} %cot_hbm.1, bf16[288,1152]{1,0:T(8,128)(2,1)} %weight.1), custom_call_target="tpu_custom_call" | custom-call | flops 10871635968 | bytes 7340032 | tf_op jit(solution)/shard_map/ffn_down_backward/pallas_call | solution.py:418
  72.0 1.6 %write_out.1 = (bf16[2,8,32,1152]{3,2,1,0:T(8,128)(2,1)}, bf16[2,8,32,1152]{3,2,1,0:T(8,128)(2,1)}, bf16[288,1152]{1,0:T(8,128)(2,1)}) custom-call(bf16[2,8,32,1152]{3,2,1,0:T(8,128)(2,1)S(1)} %get-tuple-element.9.refs_0_, bf16[2,8,32,1152]{3,2,1,0:T(8,128)(2,1)S(1)} %get-tuple-element.10.refs_1_, bf16[288,1152]{1,0:T(8,128)(2,1)S(1)} %get-tuple-element.11.refs_2_), custom_call_target="tpu_custom_call" | custom-call | tf_op jit(solution)/shard_map/write_out/pallas_call | solution.py:461
